TPU v7x, 256 devices: a whole 4x4x8 slice. The times are simulated.
256 devices in a mesh: section: 8 (over x, y_lo), tp: 32 (over y_hi, z, core).
Axes of the slice: x: 4, y: 4 (y_hi: 2, y_lo: 2; y = y_hi * 2 + y_lo), z: 8, core: 2. Of those that a mesh axis runs over, the one named last changes fastest.
Arguments:
- act_in: bfloat16 [8, 128, 4096], P('section', None, 'tp')
- grad_in: bfloat16 [8, 128, 4096], P('section', None, 'tp'), may hold values from -6 to 6
- fresh_in: bfloat16 [2, 128, 4096], P(None, None, 'tp')
- fresh_grad: bfloat16 [2, 128, 4096], P(None, None, 'tp'), may hold values from -6 to 6
- stash: bfloat16 [8, 4, 128, 4096], P('section', None, None, 'tp')
- plan: int32 [3, 8], replicated, may hold values from 0 to 3
- gain: float32 [8, 4096], P('section'), may hold values from 0.1 to 1.9
- w_gate: bfloat16 [8, 4096, 14336], P('section', None, 'tp'), may hold values from -0.09375 to 0.09375
- w_up: bfloat16 [8, 4096, 14336], P('section', None, 'tp'), may hold values from -0.09375 to 0.09375
- w_down: bfloat16 [8, 14336, 4096], P('section', 'tp'), may hold values from -0.046875 to 0.046875
Outputs:
- fwd_out: bfloat16 [8, 128, 4096], P('section', None, 'tp')
- grad_out: bfloat16 [8, 128, 4096], P('section', None, 'tp')
All inputs are finite; a program needn't handle non-finite values.
Results may differ from a plain program's by a relative error of at most 0.012.
Values may be sent and summed in bfloat16 or wider, within the bound.
A program may use at most 64 MiB of HBM per device.

v0:
```python
import jax
import jax.numpy as jnp
from jax import lax
from jax.sharding import PartitionSpec as P

EPS = 1e-05


def shifted(shard, axis, by):
    count = lax.axis_size(axis)
    pairs = [(i, i + by) for i in range(count) if 0 <= i + by < count]
    return lax.ppermute(shard, axis, pairs)


def partner_2(value, axis, apart):
    mask = 2**apart
    pairs = [(source, source ^ mask) for source in range(lax.axis_size(axis))]
    return lax.ppermute(value, axis, pairs)


def contract_last(left, right):
    return lax.dot_general(
        left, right, (((1,), (1,)), ((), ())), preferred_element_type=jnp.float32
    )


def on_device(act_in, grad_in, fresh_in, fresh_grad, stash, plan, gain, w_gate, w_up, w_down):
    n_section = lax.axis_size("section")
    section_idx = lax.axis_index("section")
    tp_idx = lax.axis_index("tp")
    width = act_in.shape[2] * lax.axis_size("tp")
    local = act_in.shape[2]
    partner = jnp.bitwise_xor(section_idx, n_section // 2)
    bit = n_section.bit_length() - 2
    gain_all = gain[0]
    gain_mine = lax.dynamic_slice_in_dim(gain_all, tp_idx * local, local, 0)
    wg = w_gate[0]
    wu = w_up[0]
    wd = w_down[0]
    held = stash[0]
    steps_total = plan.shape[0]
    acts = act_in[0]
    grads = grad_in[0]
    result_f = acts
    result_b = grads
    for step in range(steps_total):
        if step > 0:
            moved_f = shifted(result_f, "section", 1)
            moved_b = shifted(result_b, "section", -1)
            acts = jnp.where(section_idx == 0, fresh_in[step - 1], moved_f)
            grads = jnp.where(section_idx == n_section - 1, fresh_grad[step - 1], moved_b)
        slot = lax.dynamic_index_in_dim(plan[step], partner, 0, keepdims=False)
        back_in = partner_2(lax.dynamic_index_in_dim(held, slot, 0, keepdims=False), "section", bit)
        fwd32 = acts.astype(jnp.float32)
        back32 = back_in.astype(jnp.float32)
        square_f, square_b = lax.psum(
            (jnp.sum(fwd32 * fwd32, axis=-1), jnp.sum(back32 * back32, axis=-1)), "tp"
        )
        scale_f = lax.rsqrt(square_f / width + EPS)[:, None]
        scale_b = lax.rsqrt(square_b / width + EPS)[:, None]
        normed_f = (fwd32 * scale_f * gain_mine).astype(jnp.bfloat16)
        normed_b = (back32 * scale_b * gain_mine).astype(jnp.bfloat16)
        piece = lax.all_gather(normed_f, "tp", axis=1, tiled=True)
        gate = jnp.dot(piece, wg, preferred_element_type=jnp.float32)
        up = jnp.dot(piece, wu, preferred_element_type=jnp.float32)
        hidden = (jax.nn.silu(gate) * up).astype(jnp.bfloat16)
        terms = jnp.dot(hidden, wd, preferred_element_type=jnp.float32)
        down = lax.psum_scatter(terms, "tp", scatter_dimension=1, tiled=True)
        result_f = (fwd32 + down).astype(jnp.bfloat16)
        pieces = (
            lax.all_gather(normed_b, "tp", axis=1, tiled=True),
            lax.all_gather(grads, "tp", axis=1, tiled=True),
        )
        gate_b = jnp.dot(pieces[0], wg, preferred_element_type=jnp.float32)
        up_b = jnp.dot(pieces[0], wu, preferred_element_type=jnp.float32)
        grad_h = contract_last(pieces[1], wd)
        sig = jax.nn.sigmoid(gate_b)
        grad_gate = (grad_h * up_b * sig * (1.0 + gate_b * (1.0 - sig))).astype(jnp.bfloat16)
        grad_up = (grad_h * gate_b * sig).astype(jnp.bfloat16)
        norm_terms = contract_last(grad_gate, wg) + contract_last(grad_up, wu)
        norm_whole = lax.psum(norm_terms, "tp")
        back_whole = lax.all_gather(back_in, "tp", axis=1, tiled=True).astype(jnp.float32)
        inner = jnp.sum(back_whole * gain_all * norm_whole, axis=-1)
        grad_norm = lax.dynamic_slice_in_dim(norm_whole, tp_idx * local, local, 1)
        cube = scale_b * scale_b * scale_b
        result_b = (
            grads.astype(jnp.float32)
            + scale_b * gain_mine * grad_norm
            - back32 * cube * inner[:, None] / width
        ).astype(jnp.bfloat16)
    return (result_f[None], result_b[None])


def solution(mesh):
    in_specs = (
        P("section", None, "tp"),
        P("section", None, "tp"),
        P(None, None, "tp"),
        P(None, None, "tp"),
        P("section", None, None, "tp"),
        P(),
        P("section", None),
        P("section", None, "tp"),
        P("section", None, "tp"),
        P("section", "tp", None),
    )
    out_specs = (P("section", None, "tp"), P("section", None, "tp"))
    return jax.shard_map(
        on_device, mesh=mesh, in_specs=in_specs, out_specs=out_specs, check_vma=False
    )
```

profile of v0, /device:TPU:1, one launch (start us, length us, event | category | flops | bytes accessed | tf_op | source)
XLA Modules:
  0.0 2226.3 jit_solution(13607411657007269491)
XLA Ops:
  8.1 69.1 %psum.63 = f32[128]{0:T(128)S(1)} all-reduce(f32[128]{0:T(128)S(1)} %fusion.174), channel_id=1, replica_groups=mesh['section'=8,'tp'=32] {'tp'}, use_global_device_ids=true, to_apply=%region_1.2 | all-reduce | flops 128 | bytes 1024 | tf_op jit(solution)/shard_map/psum | solution.py:56
  79.4 71.4 %all-gather.14.cloned.1.call-done = bf16[128,4096]{1,0:T(8,128)(2,1)} async-done(((bf16[128,128]{1,0:T(8,128)(2,1)}), bf16[128,4096]{1,0:T(8,128)(2,1)}) %all-gather.14.cloned.1.call-update) | async-done | bytes 1048592 | tf_op jit(solution)/shard_map/all_gather | solution.py:63
  154.4 7.4 fusion.10
  161.9 111.6 %reduce-scatter.4.cloned.1.call-done = f32[128,128]{1,0:T(8,128)} async-done(((f32[128,4096]{1,0:T(8,128)}), f32[128,128]{1,0:T(8,128)}) %reduce-scatter.4.cloned.1.call-update) | async-done | bytes 65552 | tf_op jit(solution)/shard_map/reduce_scatter | solution.py:68
  277.8 71.0 %psum.64 = f32[128]{0:T(128)S(1)} all-reduce(f32[128]{0:T(128)S(1)} %get-tuple-element.8), channel_id=1, replica_groups=mesh['section'=8,'tp'=32] {'tp'}, use_global_device_ids=true, to_apply=%region_4.5 | all-reduce | flops 128 | bytes 1024 | tf_op jit(solution)/shard_map/psum | solution.py:56
  349.6 70.0 %all-gather.16.cloned.1.call-done = bf16[128,4096]{1,0:T(8,128)(2,1)} async-done(((bf16[128,128]{1,0:T(8,128)(2,1)}), bf16[128,4096]{1,0:T(8,128)(2,1)}) %all-gather.16.cloned.1.call-update) | async-done | bytes 1048592 | tf_op jit(solution)/shard_map/all_gather | solution.py:63
  423.2 7.4 fusion.8
  445.2 97.3 %reduce-scatter.6.cloned.1.call-done = f32[128,128]{1,0:T(8,128)} async-done(((f32[128,4096]{1,0:T(8,128)}), f32[128,128]{1,0:T(8,128)}) %reduce-scatter.6.cloned.1.call-update) | async-done | bytes 65552 | tf_op jit(solution)/shard_map/reduce_scatter | solution.py:68
  546.5 71.3 %all-reduce = (f32[128]{0:T(128)S(1)}, f32[128]{0:T(128)S(1)}, f32[128]{0:T(128)S(1)}, f32[128]{0:T(128)S(1)}) all-reduce(f32[128]{0:T(128)S(1)} %get-tuple-element.6, f32[128]{0:T(128)S(1)} %fusion.153, f32[128]{0:T(128)S(1)} %fusion.160, f32[128]{0:T(128)S(1)} %fusion.167), channel_id=1, replica_groups=mesh['section'=8,'tp'=32] {'tp'}, use_global_device_ids=true, to_apply=%region_7.8 | all-reduce | flops 512 | bytes 4096 | tf_op jit(solution)/shard_map/psum | solution.py:56
  623.9 68.9 %all-gather.20.cloned.1.call-done = bf16[128,4096]{1,0:T(8,128)(2,1)} async-done(((bf16[128,128]{1,0:T(8,128)(2,1)}), bf16[128,4096]{1,0:T(8,128)(2,1)}) %all-gather.20.cloned.1.call-update) | async-done | bytes 1048592 | tf_op jit(solution)/shard_map/all_gather | solution.py:71
  707.6 57.7 %all-gather.22.cloned.1.call-done = bf16[128,4096]{1,0:T(8,128)(2,1)} async-done(((bf16[128,128]{1,0:T(8,128)(2,1)}), bf16[128,4096]{1,0:T(8,128)(2,1)}) %all-gather.22.cloned.1.call-update) | async-done | bytes 1048592 | tf_op jit(solution)/shard_map/all_gather | solution.py:82
  765.3 271.4 %all-reduce.5.cloned.1.call-done = f32[128,4096]{1,0:T(8,128)} async-done(((f32[128,4096]{1,0:T(8,128)}), f32[128,4096]{1,0:T(8,128)}) %all-reduce.5.cloned.1.call-update) | async-done | bytes 2097168 | tf_op jit(solution)/shard_map/psum | solution.py:81
  1046.8 65.0 %all-gather.26.cloned.1.call-done = bf16[128,4096]{1,0:T(8,128)(2,1)} async-done(((bf16[128,128]{1,0:T(8,128)(2,1)}), bf16[128,4096]{1,0:T(8,128)(2,1)}) %all-gather.26.cloned.1.call-update) | async-done | bytes 1048592 | tf_op jit(solution)/shard_map/all_gather | solution.py:71
  1115.3 69.2 %all-gather.24.cloned.1.call-done = bf16[128,4096]{1,0:T(8,128)(2,1)} async-done(((bf16[128,128]{1,0:T(8,128)(2,1)}), bf16[128,4096]{1,0:T(8,128)(2,1)}) %all-gather.24.cloned.1.call-update) | async-done | bytes 1048592 | tf_op jit(solution)/shard_map/all_gather | solution.py:72
  1199.9 58.0 %all-gather.28.cloned.1.call-done = bf16[128,4096]{1,0:T(8,128)(2,1)} async-done(((bf16[128,128]{1,0:T(8,128)(2,1)}), bf16[128,4096]{1,0:T(8,128)(2,1)}) %all-gather.28.cloned.1.call-update) | async-done | bytes 1048592 | tf_op jit(solution)/shard_map/all_gather | solution.py:82
  1258.0 271.5 %all-reduce.7.cloned.1.call-done = f32[128,4096]{1,0:T(8,128)} async-done(((f32[128,4096]{1,0:T(8,128)}), f32[128,4096]{1,0:T(8,128)}) %all-reduce.7.cloned.1.call-update) | async-done | bytes 2097168 | tf_op jit(solution)/shard_map/psum | solution.py:81
  1538.8 64.2 %all-gather.32.cloned.1.call-done = bf16[128,4096]{1,0:T(8,128)(2,1)} async-done(((bf16[128,128]{1,0:T(8,128)(2,1)}), bf16[128,4096]{1,0:T(8,128)(2,1)}) %all-gather.32.cloned.1.call-update) | async-done | bytes 1048592 | tf_op jit(solution)/shard_map/all_gather | solution.py:71
  1606.5 69.5 %all-gather.30.cloned.1.call-done = bf16[128,4096]{1,0:T(8,128)(2,1)} async-done(((bf16[128,128]{1,0:T(8,128)(2,1)}), bf16[128,4096]{1,0:T(8,128)(2,1)}) %all-gather.30.cloned.1.call-update) | async-done | bytes 1048592 | tf_op jit(solution)/shard_map/all_gather | solution.py:72
  1680.1 6.1 fusion.27
  1690.6 58.3 %all-gather.34.cloned.1.call-done = bf16[128,4096]{1,0:T(8,128)(2,1)} async-done(((bf16[128,128]{1,0:T(8,128)(2,1)}), bf16[128,4096]{1,0:T(8,128)(2,1)}) %all-gather.34.cloned.1.call-update) | async-done | bytes 1048592 | tf_op jit(solution)/shard_map/all_gather | solution.py:82
  1748.9 271.3 %all-reduce.9.cloned.1.call-done = f32[128,4096]{1,0:T(8,128)} async-done(((f32[128,4096]{1,0:T(8,128)}), f32[128,4096]{1,0:T(8,128)}) %all-reduce.9.cloned.1.call-update) | async-done | bytes 2097168 | tf_op jit(solution)/shard_map/psum | solution.py:81
  2024.1 71.1 %all-gather.18.cloned.1.call-done = bf16[128,4096]{1,0:T(8,128)(2,1)} async-done(((bf16[128,128]{1,0:T(8,128)(2,1)}), bf16[128,4096]{1,0:T(8,128)(2,1)}) %all-gather.18.cloned.1.call-update) | async-done | bytes 1048592 | tf_op jit(solution)/shard_map/all_gather | solution.py:63
  2098.8 7.3 fusion.6
  2106.1 111.8 %reduce-scatter.8.cloned.1.call-done = f32[128,128]{1,0:T(8,128)} async-done(((f32[128,4096]{1,0:T(8,128)}), f32[128,128]{1,0:T(8,128)}) %reduce-scatter.8.cloned.1.call-update) | async-done | bytes 65552 | tf_op jit(solution)/shard_map/reduce_scatter | solution.py:68
  (140 shorter events, 108.2 us)
Async XLA Ops:
  7.2 143.7 %all-gather.14.cloned.1.call-start = ((), (), s32[]{:S(2)}) async-start(), calls=%async_computation.3 | async-start | bytes 1081344 | tf_op jit(solution)/shard_map/all_gather | solution.py:63
  79.4 194.1 %reduce-scatter.4.cloned.1.call-start = ((), (), s32[]{:S(2)}) async-start(), calls=%async_computation.4 | async-start | bytes 2162688 | tf_op jit(solution)/shard_map/reduce_scatter | solution.py:68
  161.8 257.8 %all-gather.16.cloned.1.call-start = ((), (), s32[]{:S(2)}) async-start(), calls=%async_computation.5 | async-start | bytes 1081344 | tf_op jit(solution)/shard_map/all_gather | solution.py:63
  274.4 3.4 collective-permute-start
  349.6 192.9 %reduce-scatter.6.cloned.1.call-start = ((), (), s32[]{:S(2)}) async-start(), calls=%async_computation.6 | async-start | bytes 2162688 | tf_op jit(solution)/shard_map/reduce_scatter | solution.py:68
  430.6 189.8 %all-gather.36.cloned.1.call-start = ((), (), s32[]{:S(2)}) async-start(), calls=%async_computation.20 | async-start | bytes 1081344 | tf_op jit(solution)/shard_map/all_gather | solution.py:72
  431.2 261.6 %all-gather.20.cloned.1.call-start = ((), (), s32[]{:S(2)}) async-start(), calls=%async_computation.9 | async-start | bytes 1081344 | tf_op jit(solution)/shard_map/all_gather | solution.py:71
  438.0 5.8 collective-permute-start.2
  440.8 4.3 collective-permute-start.4
  441.1 104.3 %collective-permute-start.6 = (bf16[128,128]{1,0:T(8,128)(2,1)S(1)}, bf16[128,128]{1,0:T(8,128)(2,1)S(1)}, u32[]{:S(2)}, u32[]{:S(2)}) collective-permute-start(bf16[128,128]{1,0:T(8,128)(2,1)S(1)} %get-tuple-element.10), channel_id=1, source_target_pairs={{0,128},{32,160},{64,192},{96,224},{128,0},{160,32},{192,64},{224,... | collective-permute-start | bytes 98312 | tf_op jit(solution)/shard_map/ppermute | solution.py:18
  618.5 146.9 %all-gather.22.cloned.1.call-start = ((), (), s32[]{:S(2)}) async-start(), calls=%async_computation.11 | async-start | bytes 1081344 | tf_op jit(solution)/shard_map/all_gather | solution.py:82
  619.2 417.6 %all-reduce.5.cloned.1.call-start = ((), (), s32[]{:S(2)}) async-start(), calls=%async_computation.10 | async-start | bytes 4194304 | tf_op jit(solution)/shard_map/psum | solution.py:81
  707.5 404.3 %all-gather.26.cloned.1.call-start = ((), (), s32[]{:S(2)}) async-start(), calls=%async_computation.13 | async-start | bytes 1081344 | tf_op jit(solution)/shard_map/all_gather | solution.py:71
  1040.7 143.8 %all-gather.24.cloned.1.call-start = ((), (), s32[]{:S(2)}) async-start(), calls=%async_computation.12 | async-start | bytes 1081344 | tf_op jit(solution)/shard_map/all_gather | solution.py:72
  1040.8 4.7 collective-permute-start.3
  1046.1 211.9 %all-gather.28.cloned.1.call-start = ((), (), s32[]{:S(2)}) async-start(), calls=%async_computation.15 | async-start | bytes 1081344 | tf_op jit(solution)/shard_map/all_gather | solution.py:82
  1046.8 482.7 %all-reduce.7.cloned.1.call-start = ((), (), s32[]{:S(2)}) async-start(), calls=%async_computation.14 | async-start | bytes 4194304 | tf_op jit(solution)/shard_map/psum | solution.py:81
  1199.1 403.9 %all-gather.32.cloned.1.call-start = ((), (), s32[]{:S(2)}) async-start(), calls=%async_computation.17 | async-start | bytes 1081344 | tf_op jit(solution)/shard_map/all_gather | solution.py:71
  1199.9 476.1 %all-gather.30.cloned.1.call-start = ((), (), s32[]{:S(2)}) async-start(), calls=%async_computation.16 | async-start | bytes 1081344 | tf_op jit(solution)/shard_map/all_gather | solution.py:72
  1532.7 4.7 collective-permute-start.5
  1538.0 210.9 %all-gather.34.cloned.1.call-start = ((), (), s32[]{:S(2)}) async-start(), calls=%async_computation.19 | async-start | bytes 1081344 | tf_op jit(solution)/shard_map/all_gather | solution.py:82
  1538.6 481.7 %all-reduce.9.cloned.1.call-start = ((), (), s32[]{:S(2)}) async-start(), calls=%async_computation.18 | async-start | bytes 4194304 | tf_op jit(solution)/shard_map/psum | solution.py:81
  1690.6 404.6 %all-gather.18.cloned.1.call-start = ((), (), s32[]{:S(2)}) async-start(), calls=%async_computation.7 | async-start | bytes 1081344 | tf_op jit(solution)/shard_map/all_gather | solution.py:63
  2024.1 193.9 %reduce-scatter.8.cloned.1.call-start = ((), (), s32[]{:S(2)}) async-start(), calls=%async_computation.8 | async-start | bytes 2162688 | tf_op jit(solution)/shard_map/reduce_scatter | solution.py:68
  (23 other events, 4694.3 us)
Sparse Core Ops, SparseCore 0:
  79.5 71.3 all-gather.13
  162.0 111.4 reduce-scatter.3
  349.7 69.9 all-gather.15
  430.7 111.6 reduce-scatter.5
  544.9 75.5 all-gather.35
  622.8 69.9 all-gather.19
  695.4 69.9 all-gather.21
  768.0 268.7 all-reduce.4
  1040.8 70.9 all-gather.25
  1114.6 69.9 all-gather.23
  1188.0 69.9 all-gather.27
  1260.6 268.7 all-reduce.6
  1532.0 70.9 all-gather.31
  1606.0 69.9 all-gather.29
  1679.0 69.9 all-gather.33
  1751.4 268.7 all-reduce.8
  2024.2 70.9 all-gather.17
  2106.3 111.6 reduce-scatter.7
where the time goes:
time: 2230 us
  waiting for transfers between devices  1870 us (84%)
  blocking collectives  211 us (9%)
  matrix products  87 us (4%)
    psum x3, waiting for transfers between devices, on_device(): norm_whole = lax.psum(norm_terms, 'tp')  814 us
    reduce_scatter x3, waiting for transfers between devices, on_device(): down = lax.psum_scatter(terms, 'tp', scatter_dimension=1, tiled=True)  321 us
    all_gather x3, waiting for transfers between devices, on_device(): piece = lax.all_gather(normed_f, 'tp', axis=1, tiled=True)  213 us
    psum x3, blocking collectives, on_device(): lax.psum((jnp.sum(fwd32 * fwd32, axis=-1), jnp.sum(back32 * back32, axis=...  211 us
    all_gather x3, waiting for transfers between devices, on_device(): lax.all_gather(normed_b, 'tp', axis=1, tiled=True)  198 us
    all_gather x3, waiting for transfers between devices, on_device(): lax.all_gather(back_in, 'tp', axis=1, tiled=True).astype(jnp.float32)  174 us
    all_gather x3, waiting for transfers between devices, on_device(): lax.all_gather(grads, 'tp', axis=1, tiled=True)  140 us
  transfers between devices with their start and end apart: 25, of which 23 were waited for; matrix products, arithmetic and copies ran while one was open for 3% of the time, Pallas kernels for 0%

commit v1 on v0

v1 whole, which is shorter than its diff:
```python
import functools

import jax
import jax.numpy as jnp
from jax import lax
from jax.experimental import pallas as pl
from jax.experimental.pallas import tpu as pltpu
from jax.sharding import PartitionSpec as P

EPS = 1e-05
MESH = pl.DeviceIdType.MESH
F32 = jnp.float32
BF16 = jnp.bfloat16
NT = (((1,), (1,)), ((), ()))
PARTS = 4


def dot(a, b):
    return jnp.dot(a, b, preferred_element_type=F32)


def dot_nt(a, b):
    return lax.dot_general(a, b, NT, preferred_element_type=F32)


def kernel(
    ticks,
    act,
    grad,
    fresh_f,
    fresh_b,
    stash,
    plan,
    gain,
    wg_hbm,
    wu_hbm,
    wd_hbm,
    out_f,
    out_b,
    wg,
    wu,
    wd,
    ag,
    picked,
    sib_out,
    sib_in,
    own,
    ring_out,
    ring_in,
    part_out,
    part_in,
    acc_g,
    acc_u,
    acc_h,
    ssq,
    hid,
    dgate,
    dup,
    cols,
    w_sem,
    first_s,
    first_r,
    stash_s,
    stash_r,
    ag_s,
    ag_r,
    agsib_s,
    agsib_r,
    rsib_s,
    rsib_r,
    rs_s,
    rs_r,
    sh_s,
    sh_r,
):
    sec = lax.axis_index("section")
    tp = lax.axis_index("tp")
    yh = tp // 16
    z = (tp // 2) % 8
    c = tp % 2
    width = gain.shape[1]

    def dev(s, y, zz):
        return (s, y * 16 + zz * 2 + c)

    sibling = (sec, yh * 16 + z * 2 + (1 - c))
    ring = (dev(sec, yh, (z + 1) % 8), dev(sec, yh, (z + 7) % 8))
    other_y = dev(sec, 1 - yh, z)
    partner = (sec + 4) % 8
    stash_to = [dev(partner, y, z) for y in range(2)]
    next_to = [dev((sec + 1) % 8, y, z) for y in range(2)]
    prev_to = [dev((sec + 7) % 8, y, z) for y in range(2)]

    def remote(src, dst, s_sem, r_sem, where):
        return pltpu.make_async_remote_copy(
            src_ref=src, dst_ref=dst, send_sem=s_sem, recv_sem=r_sem, device_id=where, device_id_type=MESH
        )

    loads = []
    for n, (src, dst) in enumerate(((wg_hbm, wg), (wu_hbm, wu), (wd_hbm, wd))):
        rows = dst.shape[0] // PARTS
        for p in range(PARTS):
            span = pl.ds(p * rows, rows)
            loads.append(pltpu.make_async_copy(src.at[0, span], dst.at[span], w_sem.at[n, p]))
    for load in loads:
        load.start()

    barrier = pltpu.get_barrier_semaphore()
    greet = [sibling, *ring, other_y, *stash_to, *next_to, *prev_to]
    for where in greet:
        pl.semaphore_signal(barrier, inc=1, device_id=where, device_id_type=MESH)
    ag[0, 0, c, z, yh] = act[0]
    ag[0, 1, c, z, yh] = grad[0]
    for t in range(ticks):
        picked[t] = stash[0, plan[t, partner]]
    pl.semaphore_wait(barrier, len(greet))

    first = []
    for q in range(2):
        mine = ag.at[0, q, c, z, yh]
        first.append(remote(mine, mine, first_s.at[q], first_r.at[q], other_y))
    for copy in first:
        copy.start()
    stashed = []
    for t in range(ticks):
        for y in range(2):
            stashed.append(
                remote(picked.at[t], ag.at[t, 2, c, z, yh], stash_s.at[t, y], stash_r.at[t, yh], stash_to[y])
            )
    for copy in stashed:
        copy.start()
    for q in range(2):
        theirs = ag.at[0, q, c, z, 1 - yh]
        remote(theirs, theirs, first_s.at[q], first_r.at[q], other_y).wait_recv()
    for load in loads:
        load.wait()

    def tick(t, _):
        sends = []

        def start(copy):
            copy.start()
            sends.append(copy)

        for y in range(2):
            slot = ag.at[t, 2, c, z, y]
            remote(slot, slot, stash_s.at[t, y], stash_r.at[t, y], stash_to[y]).wait_recv()

        def block_at(q, d, k, core):
            zz = (z + 7 - k) % 8 if d == 0 else (z + 1 + k) % 8
            if k == 3:
                return ag.at[t, q, core, zz, pl.ds(d, 1)]
            return ag.at[t, q, core, zz]

        def ring_send(q, d, k):
            zz = (z + 8 - k) % 8 if d == 0 else (z + k) % 8
            ref = ag.at[t, q, c, zz, pl.ds(d, 1)] if k == 3 else ag.at[t, q, c, zz]
            start(remote(ref, ref, ag_s.at[t, q, d, k], ag_r.at[t, q, d, k], ring[d]))

        def sib_send(q, slot, ref):
            start(remote(ref, ref, agsib_s.at[t, q, slot], agsib_r.at[t, q, slot], sibling))

        def sib_wait(q, slot, ref):
            remote(ref, ref, agsib_s.at[t, q, slot], agsib_r.at[t, q, slot], sibling).wait_recv()

        acc_g[...] = jnp.zeros_like(acc_g)
        acc_u[...] = jnp.zeros_like(acc_u)
        acc_h[...] = jnp.zeros_like(acc_h)
        ssq[...] = jnp.zeros_like(ssq)

        def wide(q, zz, y):
            return jnp.concatenate([ag[t, q, 0, zz, y], ag[t, q, 1, zz, y]], axis=1)

        def absorb(zz, y):
            at = pl.ds(pl.multiple_of((y * 8 + zz) * 256, 256), 256)
            x = jnp.concatenate([wide(0, zz, y), wide(2, zz, y)], axis=0).astype(F32)
            sq = x * x
            ssq[...] += sq[:, :128] + sq[:, 128:]
            xg = (x * gain[:, at]).astype(BF16)
            acc_g[...] += dot(xg, wg[at, :])
            acc_u[...] += dot(xg, wu[at, :])
            acc_h[...] += dot_nt(wide(1, zz, y), wd[:, at])

        for q in (0, 1, 2):
            for d in range(2):
                ring_send(q, d, 0)
            sib_send(q, 0, ag.at[t, q, c, z])
        for k in range(4):
            for q in (0, 1, 2):
                for d in range(2):
                    ref = block_at(q, d, k, c)
                    remote(ref, ref, ag_s.at[t, q, d, k], ag_r.at[t, q, d, k], ring[d]).wait_recv()
                    if k < 3:
                        ring_send(q, d, k + 1)
                    sib_send(q, 1 + 2 * k + d, ref)
            if k == 0:
                for q in range(3):
                    sib_wait(q, 0, ag.at[t, q, 1 - c, z])

                def own_blocks(j, _):
                    absorb(z, j)
                    return 0

                lax.fori_loop(0, 2, own_blocks, 0)
            else:
                for q in range(3):
                    for d in range(2):
                        sib_wait(q, 2 * k - 1 + d, block_at(q, d, k - 1, 1 - c))

                def far_blocks(j, _):
                    d = j // 2
                    absorb((z + 8 - k + 2 * k * d) % 8, j % 2)
                    return 0

                lax.fori_loop(0, 4, far_blocks, 0)
        for q in range(3):
            for d in range(2):
                sib_wait(q, 7 + d, block_at(q, d, 3, 1 - c))

        def last_blocks(j, _):
            absorb((z + 4) % 8, j)
            return 0

        lax.fori_loop(0, 2, last_blocks, 0)

        r = lax.rsqrt(jnp.sum(ssq[...], axis=1, keepdims=True) / width + EPS)

        def scaled(acc, lo):
            rr = r[lo : lo + 128]
            return jnp.where(rr > 0.0, rr * acc[lo : lo + 128, :], 0.0)

        gate_f = scaled(acc_g, 0)
        hid[...] = (gate_f * jax.nn.sigmoid(gate_f) * scaled(acc_u, 0)).astype(BF16)
        gate_b = scaled(acc_g, 128)
        up_b = scaled(acc_u, 128)
        sig = jax.nn.sigmoid(gate_b)
        grad_h = acc_h[...]
        dg = (grad_h * up_b * sig * (1.0 + gate_b * (1.0 - sig))).astype(BF16)
        du = (grad_h * gate_b * sig).astype(BF16)
        dgate[...] = dg
        dup[...] = du
        inner = jnp.sum(dg.astype(F32) * gate_b + du.astype(F32) * up_b, axis=1, keepdims=True)
        cols[0] = jnp.broadcast_to(r[128:], (128, 128))
        cols[1] = jnp.broadcast_to(inner / width, (128, 128))

        def terms(q, zz, y):
            at = pl.ds(pl.multiple_of((y * 8 + zz) * 256, 256), 256)
            if q == 0:
                return dot(hid[...], wd[:, at])
            dn = (dot_nt(dgate[...], wg[at, :]) + dot_nt(dup[...], wu[at, :])) * gain[:, at]
            rb = jnp.concatenate([cols[0], cols[0]], axis=1)
            cb = jnp.concatenate([cols[1], cols[1]], axis=1)
            return rb * (dn - wide(2, zz, y).astype(F32) * rb * cb)

        def produce(q, slot, zz):
            def one(y, _):
                value = terms(q, zz, y)
                lo, hi = value[:, :128], value[:, 128:]
                own[q, zz, y] = jnp.where(c == 0, lo, hi)
                sib_out[t, q, zz, y] = jnp.where(c == 0, hi, lo).astype(BF16)
                return 0

            lax.fori_loop(0, 2, one, 0)
            start(
                remote(sib_out.at[t, q, zz], sib_in.at[t, q, zz], rsib_s.at[t, q, slot], rsib_r.at[t, q, slot], sibling)
            )

        def dest(d, k):
            return (z + 4 - k) % 8 if d == 0 else (z + 4 + k) % 8

        def produce_step(k):
            for q in range(2):
                if k in (0, 4):
                    produce(q, 2 * k - (k > 0), dest(0, k))
                else:
                    for d in range(2):
                        produce(q, 2 * k - 1 + d, dest(d, k))

        def sib_ready(q, slot, zz):
            ref = sib_in.at[t, q, zz]
            remote(ref, ref, rsib_s.at[t, q, slot], rsib_r.at[t, q, slot], sibling).wait_recv()

        def local(q, zz, y):
            return own[q, zz, y] + sib_in[t, q, zz, y].astype(F32)

        def landing(q, d, k, ref):
            return ref.at[t, q, d, k, pl.ds(d, 1)] if k == 0 else ref.at[t, q, d, k]

        def ring_ready(q, d, k):
            ref = landing(q, d, k, ring_in)
            remote(ref, ref, rs_s.at[t, q, d, k], rs_r.at[t, q, d, k], ring[d]).wait_recv()

        produce_step(0)
        for k in range(4):
            produce_step(k + 1)
            for q in range(2):
                if k == 0:
                    sib_ready(q, 0, dest(0, 0))
                for d in range(2):
                    if k > 0:
                        sib_ready(q, 2 * k - 1 + d, dest(d, k))
                        ring_ready(q, d, k - 1)
                    for y in (d,) if k == 0 else (0, 1):
                        total = local(q, dest(d, k), y)
                        if k > 1 or (k == 1 and y == d):
                            total += ring_in[t, q, d, k - 1, y].astype(F32)
                        ring_out[t, q, d, k, y] = total.astype(BF16)
                    start(
                        remote(
                            landing(q, d, k, ring_out),
                            landing(q, d, k, ring_in),
                            rs_s.at[t, q, d, k],
                            rs_r.at[t, q, d, k],
                            ring[d],
                        )
                    )
        for q in range(2):
            sib_ready(q, 7, z)
            for d in range(2):
                ring_ready(q, d, 3)

        def summed(q, y):
            total = local(q, z, y) + ring_in[t, q, 0, 3, y].astype(F32) + ring_in[t, q, 1, 3, y].astype(F32)
            return total + jnp.where(y == yh, ag[t, q, c, z, yh].astype(F32), 0.0)

        @pl.when(t < ticks - 1)
        def _():
            moves = []
            for q, edge, fresh, to in ((0, 7, fresh_f, next_to), (1, 0, fresh_b, prev_to)):
                for y in range(2):
                    new = jnp.where(y == yh, fresh[t].astype(F32), 0.0)
                    part_out[t, q, y] = jnp.where(sec == edge, new, summed(q, y)).astype(BF16)
                for y in range(2):
                    copy = remote(
                        part_out.at[t, q], part_in.at[t, q, yh], sh_s.at[t, q, y], sh_r.at[t, q, yh], to[y]
                    )
                    copy.start()
                    moves.append(copy)
            for copy in sends:
                copy.wait_send()
            for q, to in ((0, next_to), (1, prev_to)):
                for y in range(2):
                    ref = part_in.at[t, q, y]
                    remote(ref, ref, sh_s.at[t, q, y], sh_r.at[t, q, y], to[y]).wait_recv()
                for y in range(2):
                    ag[t + 1, q, c, z, y] = (
                        part_in[t, q, 0, y].astype(F32) + part_in[t, q, 1, y].astype(F32)
                    ).astype(BF16)
            for copy in moves:
                copy.wait_send()

        @pl.when(t == ticks - 1)
        def _():
            moves = []
            for q in range(2):
                part_out[t, q, 1 - yh] = summed(q, 1 - yh).astype(BF16)
                copy = remote(
                    part_out.at[t, q, 1 - yh],
                    part_in.at[t, q, yh, 1 - yh],
                    sh_s.at[t, q, 0],
                    sh_r.at[t, q, yh],
                    other_y,
                )
                copy.start()
                moves.append(copy)
            for copy in sends:
                copy.wait_send()
            for q, out in ((0, out_f), (1, out_b)):
                ref = part_in.at[t, q, 1 - yh, yh]
                remote(ref, ref, sh_s.at[t, q, 0], sh_r.at[t, q, 1 - yh], other_y).wait_recv()
                out[0] = (summed(q, yh) + part_in[t, q, 1 - yh, yh].astype(F32)).astype(BF16)
            for copy in moves:
                copy.wait_send()

        return 0

    lax.fori_loop(0, ticks, tick, 0)
    for copy in first + stashed:
        copy.wait_send()


def on_device(act_in, grad_in, fresh_in, fresh_grad, stash, plan, gain, w_gate, w_up, w_down):
    ticks = plan.shape[0]
    rows, cols = act_in.shape[1:]
    width, units = w_gate.shape[1:]
    tile = (rows, cols)
    vmem = pl.BlockSpec(memory_space=pltpu.VMEM)
    anywhere = pl.BlockSpec(memory_space=pl.ANY)
    dma = pltpu.SemaphoreType.DMA
    return pl.pallas_call(
        functools.partial(kernel, ticks),
        out_shape=[jax.ShapeDtypeStruct((1,) + tile, BF16)] * 2,
        in_specs=[vmem] * 5 + [pl.BlockSpec(memory_space=pltpu.SMEM), vmem] + [anywhere] * 3,
        out_specs=[vmem] * 2,
        scratch_shapes=[
            pltpu.VMEM((width, units), BF16),
            pltpu.VMEM((width, units), BF16),
            pltpu.VMEM((units, width), BF16),
            pltpu.VMEM((ticks, 3, 2, 8, 2) + tile, BF16),
            pltpu.VMEM((ticks,) + tile, BF16),
            pltpu.VMEM((ticks, 2, 8, 2) + tile, BF16),
            pltpu.VMEM((ticks, 2, 8, 2) + tile, BF16),
            pltpu.VMEM((2, 8, 2) + tile, F32),
            pltpu.VMEM((ticks, 2, 2, 4, 2) + tile, BF16),
            pltpu.VMEM((ticks, 2, 2, 4, 2) + tile, BF16),
            pltpu.VMEM((ticks, 2, 2) + tile, BF16),
            pltpu.VMEM((ticks, 2, 2, 2) + tile, BF16),
            pltpu.VMEM((2 * rows, units), F32),
            pltpu.VMEM((2 * rows, units), F32),
            pltpu.VMEM((rows, units), F32),
            pltpu.VMEM((2 * rows, 128), F32),
            pltpu.VMEM((rows, units), BF16),
            pltpu.VMEM((rows, units), BF16),
            pltpu.VMEM((rows, units), BF16),
            pltpu.VMEM((2, rows, 128), F32),
            dma((3, PARTS)),
            dma((2,)),
            dma((2,)),
            dma((ticks, 2)),
            dma((ticks, 2)),
            dma((ticks, 3, 2, 4)),
            dma((ticks, 3, 2, 4)),
            dma((ticks, 3, 9)),
            dma((ticks, 3, 9)),
            dma((ticks, 2, 8)),
            dma((ticks, 2, 8)),
            dma((ticks, 2, 2, 4)),
            dma((ticks, 2, 2, 4)),
            dma((ticks, 2, 2)),
            dma((ticks, 2, 2)),
        ],
        compiler_params=pltpu.CompilerParams(
            collective_id=0, has_side_effects=True, vmem_limit_bytes=56 * 2**20
        ),
        name="relay",
    )(act_in, grad_in, fresh_in, fresh_grad, stash, plan, gain, w_gate, w_up, w_down)


def solution(mesh):
    in_specs = (
        P("section", None, "tp"),
        P("section", None, "tp"),
        P(None, None, "tp"),
        P(None, None, "tp"),
        P("section", None, None, "tp"),
        P(),
        P("section", None),
        P("section", None, "tp"),
        P("section", None, "tp"),
        P("section", "tp", None),
    )
    out_specs = (P("section", None, "tp"), P("section", None, "tp"))
    return jax.shard_map(on_device, mesh=mesh, in_specs=in_specs, out_specs=out_specs, check_vma=False)
```

time: 2230 us -> 170 us (0.08)
  waiting for transfers between devices: 1870 us -> 0 us
  blocking collectives: 211 us -> 0 us
  Pallas kernels: 0 us -> 151 us
  matrix products: 87 us -> 0 us
    psum x3 -> x0, waiting for transfers between devices: 814 us -> none  [on_device(): norm_whole = lax.psum(norm_terms, 'tp')]
    all_gather x12 -> x0, waiting for transfers between devices: 724 us -> none  [the longest x3 213 us: on_device(): piece = lax.all_gather(normed_f, 'tp', axis=1, tiled=True)]
    reduce_scatter x3 -> x0, waiting for transfers between devices: 321 us -> none  [on_device(): down = lax.psum_scatter(terms, 'tp', scatter_dimension=1, tiled=True)]
    psum x3 -> x0, blocking collectives: 211 us -> none  [on_device(): lax.psum((jnp.sum(fwd32 * fwd32, axis=-1), jnp.sum(back32 * back32, axis=...]
    pallas_call x0 -> x1, Pallas kernels: none -> 151 us  [on_device(): pl.pallas_call(functools.partial(kernel, ticks), out_shape=[jax.ShapeDtyp...]
    dot_general x18 -> x0, matrix products: 87 us -> none  [the longest x9 43 us: contract_last(): lax.dot_general(left, right, (((1,), (1,)), ((), ())), preferred_element_...]
  transfers between devices with their start and end apart: 25 -> 0, of which waited for: 23 -> 0; matrix products, arithmetic and copies ran while one was open for 3% -> 0% of each run, Pallas kernels for 0% -> 0%
where the time goes in v1:
time: 170 us; the launch traced here: 167 us
  Pallas kernels  151 us (89%)
  local copies, waits for them, and re-layouts  15.6 us (9%)
    pallas_call x1, Pallas kernels, on_device(): pl.pallas_call(functools.partial(kernel, ticks), out_shape=[jax.ShapeDtyp...  151 us
    unnamed x4, local copies, waits for them, and re-layouts  15.6 us

profile of v1, /device:TPU:1, one launch (start us, length us, event | category | flops | bytes accessed | tf_op | source)
XLA Modules:
  0.0 166.9 jit_solution(10756777190496183643)
XLA Ops:
  0.6 6.4 %copy.12.wg_hbm = bf16[1,4096,448]{2,1,0:T(8,128)(2,1)} copy(bf16[1,4096,448]{1,2,0:T(8,128)(2,1)} %param.17) | data formatting | bytes 7340032 | tf_op args[7]
  7.0 6.5 %copy.13.wu_hbm = bf16[1,4096,448]{2,1,0:T(8,128)(2,1)} copy(bf16[1,4096,448]{1,2,0:T(8,128)(2,1)} %param.18) | data formatting | bytes 7340032 | tf_op args[8]
  13.5 150.7 %relay.1 = (bf16[1,128,128]{2,1,0:T(8,128)(2,1)}, bf16[1,128,128]{2,1,0:T(8,128)(2,1)}) custom-call(bf16[1,128,128]{2,1,0:T(8,128)(2,1)} %act.1, bf16[1,128,128]{2,1,0:T(8,128)(2,1)} %grad.1, bf16[2,128,128]{2,1,0:T(8,128)(2,1)} %fresh_f.1, bf16[2,128,128]{2,1,0:T(8,128)(2,1)} %fresh_b.1, bf16[1,4,128,128]{3,2,1,0:T(8,128)(2,1)} %stash.1, s32[3,8]{1,0:T(4,128)} %plan.1, ...), custom_call_target="tpu_custom_call" | custom-call | tf_op jit(solution)/shard_map/relay/pallas_call | solution.py:390
  164.2 1.4 copy.16
  165.6 1.4 copy.17

commit v2 on v1

v2 whole, which is shorter than its diff:
```python
import functools

import jax
import jax.numpy as jnp
from jax import lax
from jax.experimental import pallas as pl
from jax.experimental.pallas import tpu as pltpu
from jax.sharding import PartitionSpec as P

EPS = 1e-05
MESH = pl.DeviceIdType.MESH
F32 = jnp.float32
BF16 = jnp.bfloat16
NT = (((1,), (1,)), ((), ()))
PARTS = 4


def dot(a, b):
    return jnp.dot(a, b, preferred_element_type=F32)


def dot_nt(a, b):
    return lax.dot_general(a, b, NT, preferred_element_type=F32)


def kernel(
    ticks,
    act,
    grad,
    fresh_f,
    fresh_b,
    stash,
    plan,
    gain,
    wg_hbm,
    wu_hbm,
    wd_hbm,
    outs,
    wgu,
    wd,
    ag,
    sg,
    picked,
    sib_out,
    sib_in,
    own,
    ring_out,
    ring_in,
    part_out,
    part_in,
    acc_g,
    acc_u,
    acc_h,
    ssq,
    hid,
    dgu,
    cols,
    w_sem,
    first_s,
    first_r,
    stash_s,
    stash_r,
    spread_s,
    spread_r,
    cross_s,
    cross_r,
    pair_s,
    pair_r,
    ag_s,
    ag_r,
    agsib_s,
    agsib_r,
    rsib_s,
    rsib_r,
    rs_s,
    rs_r,
    sh_s,
    sh_r,
):
    sec = lax.axis_index("section")
    tp = lax.axis_index("tp")
    yh = tp // 16
    z = (tp // 2) % 8
    c = tp % 2
    width = gain.shape[1]

    def dev(s, y, zz):
        return (s, y * 16 + zz * 2 + c)

    sibling = (sec, yh * 16 + z * 2 + (1 - c))
    ring = (dev(sec, yh, (z + 1) % 8), dev(sec, yh, (z + 7) % 8))
    other_y = dev(sec, 1 - yh, z)
    partner = (sec + 4) % 8
    stash_to = dev(partner, yh, z)
    along = [dev(sec, yh, (z + i) % 8) for i in range(1, 8)]
    next_to = [dev((sec + 1) % 8, y, z) for y in range(2)]
    prev_to = [dev((sec + 7) % 8, y, z) for y in range(2)]

    def remote(src, dst, s_sem, r_sem, where):
        return pltpu.make_async_remote_copy(
            src_ref=src, dst_ref=dst, send_sem=s_sem, recv_sem=r_sem, device_id=where, device_id_type=MESH
        )

    loads = []
    units = wd.shape[0]
    rows = units // PARTS
    for n, (src, dst, base) in enumerate(((wg_hbm, wgu, 0), (wu_hbm, wgu, units), (wd_hbm, wd, 0))):
        for p in range(PARTS):
            span = pl.ds(p * rows, rows)
            loads.append(pltpu.make_async_copy(src.at[0, span], dst.at[pl.ds(base + p * rows, rows)], w_sem.at[n, p]))
    for load in loads:
        load.start()

    barrier = pltpu.get_barrier_semaphore()
    greet = [sibling, *along, other_y, stash_to, *next_to, *prev_to]
    for where in greet:
        pl.semaphore_signal(barrier, inc=1, device_id=where, device_id_type=MESH)
    ag[0, 0, c, z, yh] = act[0]
    ag[0, 1, c, z, yh] = grad[0]
    for t in range(ticks):
        picked[t] = stash[0, plan[t, partner]]
    pl.semaphore_wait(barrier, len(greet))

    first = []
    for q in range(2):
        mine = ag.at[0, q, c, z, yh]
        first.append(remote(mine, mine, first_s.at[q], first_r.at[q], other_y))
    for copy in first:
        copy.start()
    stashed = [remote(picked.at[t], sg.at[t, c, yh, z], stash_s.at[t], stash_r.at[t], stash_to) for t in range(ticks)]
    for copy in stashed:
        copy.start()

    def stash_ready(t):
        ref = sg.at[t, c, yh, z]
        remote(ref, ref, stash_s.at[t], stash_r.at[t], stash_to).wait_recv()

    def spread(t, i, zz):
        ref = sg.at[t, c, yh, zz]
        return remote(ref, ref, spread_s.at[t, i], spread_r.at[t, i], along[i])

    def spread_start(t):
        stash_ready(t)
        for i in (3, 4, 2, 5, 1, 6, 0):
            spread(t, i, z).start()

    def cross(t, y):
        ref = sg.at[t, c, y]
        return remote(ref, ref, cross_s.at[t], cross_r.at[t], other_y)

    def cross_start(t):
        for i in range(7):
            spread(t, i, (z + 7 - i) % 8).wait_recv()
        cross(t, yh).start()

    def pair(t, core):
        ref = sg.at[t, core]
        return remote(ref, ref, pair_s.at[t], pair_r.at[t], sibling)

    def pair_start(t):
        cross(t, 1 - yh).wait_recv()
        pair(t, c).start()

    def spread_sent(t):
        for i in range(7):
            spread(t, i, z).wait_send()
        cross(t, yh).wait_send()


    def first_ready(q):
        theirs = ag.at[0, q, c, z, 1 - yh]
        remote(theirs, theirs, first_s.at[q], first_r.at[q], other_y).wait_recv()

    def f_move(t, y, source):
        return remote(part_out.at[t, 0], part_in.at[t, 0, source], sh_s.at[t, 0, y], sh_r.at[t, 0, source], next_to[y])

    def b_move(t, y, source):
        return remote(part_out.at[t, 1], part_in.at[t, 1, source], sh_s.at[t, 1, y], sh_r.at[t, 1, source], prev_to[y])

    def tick(t, _):
        sends = []

        def start(copy):
            copy.start()
            sends.append(copy)

        def behind(d, k):
            return (z + 8 - k) % 8 if d == 0 else (z + k) % 8

        def halves(k, d):
            return (d,) if k == 3 else (0, 1)

        def ring_copy(q, d, k, y, zz):
            ref = ag.at[t, q, c, zz, y]
            return remote(ref, ref, ag_s.at[t, q, d, k, y], ag_r.at[t, q, d, k, y], ring[d])

        def sib_copy(q, slot, zz, core):
            ref = ag.at[t, q, core, zz]
            return remote(ref, ref, agsib_s.at[t, q, slot], agsib_r.at[t, q, slot], sibling)

        def sib_wait(slot, zz):
            for q in range(2):
                sib_copy(q, slot, zz, 1 - c).wait_recv()

        def leave(q):
            for d in range(2):
                start(ring_copy(q, d, 0, yh, z))
            pl.when(t == 0)(lambda: first_ready(q))
            for d in range(2):
                start(ring_copy(q, d, 0, 1 - yh, z))
            start(sib_copy(q, 0, z, c))

        @pl.when(t > 0)
        def _():
            f_move(t - 1, 0, 0).wait_recv()
            f_move(t - 1, 1, 1).wait_recv()
            for y in range(2):
                both = part_in[t - 1, 0, 0, y].astype(F32) + part_in[t - 1, 0, 1, y].astype(F32)
                ag[t, 0, c, z, y] = both.astype(BF16)

        leave(0)

        @pl.when(t > 0)
        def _():
            b_move(t - 1, 0, 0).wait_recv()
            b_move(t - 1, 1, 1).wait_recv()
            for y in range(2):
                both = part_in[t - 1, 1, 0, y].astype(F32) + part_in[t - 1, 1, 1, y].astype(F32)
                ag[t, 1, c, z, y] = both.astype(BF16)

        leave(1)

        acc_g[...] = jnp.zeros_like(acc_g)
        acc_u[...] = jnp.zeros_like(acc_u)
        acc_h[...] = jnp.zeros_like(acc_h)
        ssq[...] = jnp.zeros_like(ssq)

        def wide(q, zz, y):
            return jnp.concatenate([ag[t, q, 0, zz, y], ag[t, q, 1, zz, y]], axis=1)

        def held(zz, y):
            return jnp.concatenate([sg[t, 0, y, zz], sg[t, 1, y, zz]], axis=1)

        def enter(lo, block, zz, also):
            rows = pl.ds(lo, 128)
            g_sum, u_sum, h_sum, q_sum = 0.0, 0.0, 0.0, 0.0
            for y in range(2):
                at = pl.ds(pl.multiple_of((y * 8 + zz) * 256, 256), 256)
                x = block(zz, y).astype(F32)
                sq = x * x
                q_sum += sq[:, :128] + sq[:, 128:]
                xg = (x * gain[:, at]).astype(BF16)
                g_sum += dot_nt(xg, wgu[:units, at])
                u_sum += dot_nt(xg, wgu[units:, at])
                if also:
                    h_sum += dot_nt(wide(1, zz, y), wd[:, at])
            ssq[rows, :] += q_sum
            acc_g[rows, :] += g_sum
            acc_u[rows, :] += u_sum
            if also:
                acc_h[...] += h_sum

        def absorb(zz):
            enter(0, functools.partial(wide, 0), zz, True)

        def absorb_held(first, count):
            def one(j, _):
                enter(128, held, (z + j) % 8, False)
                return 0

            lax.fori_loop(first, first + count, one, 0)

        @pl.when(t == 0)
        def _():
            spread_start(0)
            for load in loads:
                load.wait()

        @pl.when(t > 0)
        def _():
            f_move(t - 1, 0, 0).wait_send()
            f_move(t - 1, 1, 0).wait_send()
            b_move(t - 1, 0, 0).wait_send()
            b_move(t - 1, 1, 0).wait_send()
            pair(t, c).wait_send()
            pair(t, 1 - c).wait_recv()
            absorb_held(0, 3)

        sib_wait(0, z)

        def arrivals(q, k):
            for y in range(2):
                for d in range(2):
                    if y in halves(k, d):
                        zz = behind(d, k + 1)
                        ring_copy(q, d, k, y, zz).wait_recv()
                        if k < 3 and y in halves(k + 1, d):
                            start(ring_copy(q, d, k + 1, y, zz))
            if k == 3:
                start(sib_copy(q, 7, (z + 4) % 8, c))
            else:
                for d in range(2):
                    start(sib_copy(q, 1 + 2 * k + d, behind(d, k + 1), c))

        for k in range(4):
            for q in range(2):
                arrivals(q, k)
                if k > 0:
                    sib_wait(2 * k - 1 + q, behind(q, k))
                    absorb(behind(q, k))
                elif q == 0:
                    absorb(z)
                else:

                    @pl.when(t > 0)
                    def _():
                        absorb_held(3, 5)

            if k == 1:
                pl.when(t == 0)(lambda: cross_start(0))
            if k == 3:
                pl.when(t == 0)(lambda: pair_start(0))
        pl.when(t < ticks - 1)(lambda: spread_start(t + 1))
        sib_wait(7, (z + 4) % 8)
        absorb((z + 4) % 8)

        def scaled(lo):
            rows = pl.ds(lo, 128)
            r = lax.rsqrt(jnp.sum(ssq[rows, :], axis=1, keepdims=True) / width + EPS)
            gate = jnp.where(r > 0.0, r * acc_g[rows, :], 0.0)
            up = jnp.where(r > 0.0, r * acc_u[rows, :], 0.0)
            return r, gate, up

        def hidden_forward():
            _, gate, up = scaled(0)
            hid[...] = (gate * jax.nn.sigmoid(gate) * up).astype(BF16)

        def hidden_backward():
            r, gate, up = scaled(128)
            sig = jax.nn.sigmoid(gate)
            grad_h = acc_h[...]
            dg = (grad_h * up * sig * (1.0 + gate * (1.0 - sig))).astype(BF16)
            du = (grad_h * gate * sig).astype(BF16)
            dgu[...] = jnp.concatenate([dg, du], axis=1)
            inner = jnp.sum(dg.astype(F32) * gate + du.astype(F32) * up, axis=1, keepdims=True)
            cols[0] = jnp.broadcast_to(r, (128, 128))
            cols[1] = jnp.broadcast_to(inner / width, (128, 128))

        def terms(q, zz, y):
            at = pl.ds(pl.multiple_of((y * 8 + zz) * 256, 256), 256)
            if q == 0:
                return dot(hid[...], wd[:, at])
            dn = dot(dgu[...], wgu[:, at]) * gain[:, at]
            rb = jnp.concatenate([cols[0], cols[0]], axis=1)
            cb = jnp.concatenate([cols[1], cols[1]], axis=1)
            return rb * (dn - held(zz, y).astype(F32) * rb * cb)

        def produce(q, slot, zz):
            def one(y, _):
                value = terms(q, zz, y)
                lo, hi = value[:, :128], value[:, 128:]
                own[q, zz, y] = jnp.where(c == 0, lo, hi)
                sib_out[t, q, zz, y] = jnp.where(c == 0, hi, lo).astype(BF16)
                return 0

            lax.fori_loop(0, 2, one, 0)
            start(
                remote(sib_out.at[t, q, zz], sib_in.at[t, q, zz], rsib_s.at[t, q, slot], rsib_r.at[t, q, slot], sibling)
            )

        def dest(d, k):
            return (z + 4 - k) % 8 if d == 0 else (z + 4 + k) % 8

        def produce_step(q, k):
            if k in (0, 4):
                produce(q, 2 * k - (k > 0), dest(0, k))
            else:
                for d in range(2):
                    produce(q, 2 * k - 1 + d, dest(d, k))

        def sib_ready(q, slot, zz):
            ref = sib_in.at[t, q, zz]
            remote(ref, ref, rsib_s.at[t, q, slot], rsib_r.at[t, q, slot], sibling).wait_recv()

        def local(q, zz, y):
            return own[q, zz, y] + sib_in[t, q, zz, y].astype(F32)

        def ring_sum(q, d, k, y):
            return remote(
                ring_out.at[t, q, d, k, y],
                ring_in.at[t, q, d, k, y],
                rs_s.at[t, q, d, k, y],
                rs_r.at[t, q, d, k, y],
                ring[d],
            )

        def pass_on(q, k):
            if k == 0:
                sib_ready(q, 0, dest(0, 0))
            else:
                for d in range(2):
                    sib_ready(q, 2 * k - 1 + d, dest(d, k))
            for y in range(2):
                for d in range(2):
                    if k == 0 and y != d:
                        continue
                    total = local(q, dest(d, k), y)
                    if k > 1 or (k == 1 and y == d):
                        ring_sum(q, d, k - 1, y).wait_recv()
                        total += ring_in[t, q, d, k - 1, y].astype(F32)
                    ring_out[t, q, d, k, y] = total.astype(BF16)
                    start(ring_sum(q, d, k, y))

        hidden_forward()
        produce_step(0, 0)

        @pl.when(t == 0)
        def _():
            pair(0, 1 - c).wait_recv()
            pair(0, c).wait_send()
            absorb_held(0, 8)

        hidden_backward()
        produce_step(1, 0)
        for k in range(4):
            for q in range(2):
                pass_on(q, k)
                produce_step(q, k + 1)
            if k == 1:
                pl.when(t < ticks - 1)(lambda: cross_start(t + 1))

        def finish(q):
            sib_ready(q, 7, z)
            for y in range(2):
                for d in range(2):
                    ring_sum(q, d, 3, y).wait_recv()

        def summed(q, y):
            total = local(q, z, y) + ring_in[t, q, 0, 3, y].astype(F32) + ring_in[t, q, 1, 3, y].astype(F32)
            return total + jnp.where(y == yh, ag[t, q, c, z, yh].astype(F32), 0.0)

        @pl.when(t < ticks - 1)
        def _():
            for q, edge, fresh, move in ((0, 7, fresh_f, f_move), (1, 0, fresh_b, b_move)):
                finish(q)
                for y in range(2):
                    new = jnp.where(y == yh, fresh[t].astype(F32), 0.0)
                    part_out[t, q, y] = jnp.where(sec == edge, new, summed(q, y)).astype(BF16)
                for y in range(2):
                    move(t, y, yh).start()
            pair_start(t + 1)
            for copy in sends:
                copy.wait_send()
            spread_sent(t + 1)

        @pl.when(t == ticks - 1)
        def _():
            moves = []
            for q in range(2):
                finish(q)
                part_out[t, q, 1 - yh] = summed(q, 1 - yh).astype(BF16)
                copy = remote(
                    part_out.at[t, q, 1 - yh],
                    part_in.at[t, q, yh, 1 - yh],
                    sh_s.at[t, q, 0],
                    sh_r.at[t, q, yh],
                    other_y,
                )
                copy.start()
                moves.append(copy)
            for copy in sends:
                copy.wait_send()
            for q in range(2):
                ref = part_in.at[t, q, 1 - yh, yh]
                remote(ref, ref, sh_s.at[t, q, 0], sh_r.at[t, q, 1 - yh], other_y).wait_recv()
                outs[q] = (summed(q, yh) + part_in[t, q, 1 - yh, yh].astype(F32)).astype(BF16)
            for copy in moves:
                copy.wait_send()

        return 0

    lax.fori_loop(0, ticks, tick, 0)
    for copy in first + stashed:
        copy.wait_send()
    spread_sent(0)


def on_device(act_in, grad_in, fresh_in, fresh_grad, stash, plan, gain, w_gate, w_up, w_down):
    ticks = plan.shape[0]
    rows, cols = act_in.shape[1:]
    width, units = w_gate.shape[1:]
    tile = (rows, cols)
    vmem = pl.BlockSpec(memory_space=pltpu.VMEM)
    anywhere = pl.BlockSpec(memory_space=pl.ANY)
    dma = pltpu.SemaphoreType.DMA
    both = pl.pallas_call(
        functools.partial(kernel, ticks),
        out_shape=jax.ShapeDtypeStruct((2,) + tile, BF16),
        in_specs=[vmem] * 5 + [pl.BlockSpec(memory_space=pltpu.SMEM), vmem] + [anywhere] * 3,
        out_specs=vmem,
        scratch_shapes=[
            pltpu.VMEM((2 * units, width), BF16),
            pltpu.VMEM((units, width), BF16),
            pltpu.VMEM((ticks, 2, 2, 8, 2) + tile, BF16),
            pltpu.VMEM((ticks, 2, 2, 8) + tile, BF16),
            pltpu.VMEM((ticks,) + tile, BF16),
            pltpu.VMEM((ticks, 2, 8, 2) + tile, BF16),
            pltpu.VMEM((ticks, 2, 8, 2) + tile, BF16),
            pltpu.VMEM((2, 8, 2) + tile, F32),
            pltpu.VMEM((ticks, 2, 2, 4, 2) + tile, BF16),
            pltpu.VMEM((ticks, 2, 2, 4, 2) + tile, BF16),
            pltpu.VMEM((ticks, 2, 2) + tile, BF16),
            pltpu.VMEM((ticks, 2, 2, 2) + tile, BF16),
            pltpu.VMEM((2 * rows, units), F32),
            pltpu.VMEM((2 * rows, units), F32),
            pltpu.VMEM((rows, units), F32),
            pltpu.VMEM((2 * rows, 128), F32),
            pltpu.VMEM((rows, units), BF16),
            pltpu.VMEM((rows, 2 * units), BF16),
            pltpu.VMEM((2, rows, 128), F32),
            dma((3, PARTS)),
            dma((2,)),
            dma((2,)),
            dma((ticks,)),
            dma((ticks,)),
            dma((ticks, 7)),
            dma((ticks, 7)),
            dma((ticks,)),
            dma((ticks,)),
            dma((ticks,)),
            dma((ticks,)),
            dma((ticks, 2, 2, 4, 2)),
            dma((ticks, 2, 2, 4, 2)),
            dma((ticks, 2, 8)),
            dma((ticks, 2, 8)),
            dma((ticks, 2, 8)),
            dma((ticks, 2, 8)),
            dma((ticks, 2, 2, 4, 2)),
            dma((ticks, 2, 2, 4, 2)),
            dma((ticks, 2, 2)),
            dma((ticks, 2, 2)),
        ],
        compiler_params=pltpu.CompilerParams(
            collective_id=0, has_side_effects=True, vmem_limit_bytes=56 * 2**20
        ),
        name="relay",
    )(act_in, grad_in, fresh_in, fresh_grad, stash, plan, gain, jnp.swapaxes(w_gate, 1, 2), jnp.swapaxes(w_up, 1, 2), w_down)
    return both[:1], both[1:]


def solution(mesh):
    in_specs = (
        P("section", None, "tp"),
        P("section", None, "tp"),
        P(None, None, "tp"),
        P(None, None, "tp"),
        P("section", None, None, "tp"),
        P(),
        P("section", None),
        P("section", None, "tp"),
        P("section", None, "tp"),
        P("section", "tp", None),
    )
    out_specs = (P("section", None, "tp"), P("section", None, "tp"))
    return jax.shard_map(on_device, mesh=mesh, in_specs=in_specs, out_specs=out_specs, check_vma=False)
```

time: 170 us -> 148 us (0.87); the launches traced: 167 us -> 148 us
  local copies, waits for them, and re-layouts: 15.6 us -> 1.4 us
  Pallas kernels: 151 us -> 146 us
    unnamed x4 -> x0, local copies, waits for them, and re-layouts: 15.6 us -> none
    pallas_call x1, Pallas kernels: 151 us -> 146 us  [on_device(): pl.pallas_call(functools.partial(kernel, ticks), out_shape=jax.ShapeDtype...]
where the time goes in v2:
time: 148 us
  Pallas kernels  146 us (99%)
    pallas_call x1, Pallas kernels, on_device(): pl.pallas_call(functools.partial(kernel, ticks), out_shape=jax.ShapeDtype...  146 us

profile of v2, /device:TPU:1, one launch (start us, length us, event | category | flops | bytes accessed | tf_op | source)
XLA Modules:
  0.0 148.3 jit_solution(3399574825646558445)
XLA Ops:
  0.6 146.2 %relay.1 = bf16[2,128,128]{2,1,0:T(8,128)(2,1)} custom-call(bf16[1,128,128]{2,1,0:T(8,128)(2,1)} %act.1, bf16[1,128,128]{2,1,0:T(8,128)(2,1)} %grad.1, bf16[2,128,128]{2,1,0:T(8,128)(2,1)} %fresh_f.1, bf16[2,128,128]{2,1,0:T(8,128)(2,1)} %fresh_b.1, bf16[1,4,128,128]{3,2,1,0:T(8,128)(2,1)} %stash.1, s32[3,8]{1,0:T(4,128)} %plan.1, f32[1,4096]{1,0:T(1,128)} %gain.1, ...), custom_call_target="tpu_custom_call" | custom-call | tf_op jit(solution)/shard_map/relay/pallas_call | solution.py:496
  146.9 1.4 fusion

commit v3 on v2

--- a/solution.py
+++ b/solution.py
@@ -27,15 +27,20 @@
     ticks,
     act,
     grad,
-    fresh_f,
-    fresh_b,
-    stash,
+    fresh_f_hbm,
+    fresh_b_hbm,
+    stash_hbm,
     plan,
-    gain,
+    gain_hbm,
     wg_hbm,
     wu_hbm,
     wd_hbm,
     outs,
+    fresh_f,
+    fresh_b,
+    stash,
+    gain,
+    small_sem,
     wgu,
     wd,
     ag,
@@ -101,6 +106,22 @@
             src_ref=src, dst_ref=dst, send_sem=s_sem, recv_sem=r_sem, device_id=where, device_id_type=MESH
         )
 
+    smalls = [
+        pltpu.make_async_copy(src, dst, small_sem.at[n])
+        for n, (src, dst) in enumerate(
+            (
+                (act.at[0], ag.at[0, 0, c, z, yh]),
+                (grad.at[0], ag.at[0, 1, c, z, yh]),
+                (stash_hbm.at[0], stash),
+                (fresh_f_hbm, fresh_f),
+                (fresh_b_hbm, fresh_b),
+                (gain_hbm, gain),
+            )
+        )
+    ]
+    for copy in smalls:
+        copy.start()
+
     loads = []
     units = wd.shape[0]
     rows = units // PARTS
@@ -115,10 +136,10 @@
     greet = [sibling, *along, other_y, stash_to, *next_to, *prev_to]
     for where in greet:
         pl.semaphore_signal(barrier, inc=1, device_id=where, device_id_type=MESH)
-    ag[0, 0, c, z, yh] = act[0]
-    ag[0, 1, c, z, yh] = grad[0]
+    for copy in smalls:
+        copy.wait()
     for t in range(ticks):
-        picked[t] = stash[0, plan[t, partner]]
+        picked[t] = stash[plan[t, partner]]
     pl.semaphore_wait(barrier, len(greet))
 
     first = []
@@ -492,13 +513,19 @@
     tile = (rows, cols)
     vmem = pl.BlockSpec(memory_space=pltpu.VMEM)
     anywhere = pl.BlockSpec(memory_space=pl.ANY)
+    hbm = pl.BlockSpec(memory_space=pltpu.HBM)
     dma = pltpu.SemaphoreType.DMA
     both = pl.pallas_call(
         functools.partial(kernel, ticks),
         out_shape=jax.ShapeDtypeStruct((2,) + tile, BF16),
-        in_specs=[vmem] * 5 + [pl.BlockSpec(memory_space=pltpu.SMEM), vmem] + [anywhere] * 3,
+        in_specs=[hbm] * 5 + [pl.BlockSpec(memory_space=pltpu.SMEM), hbm] + [anywhere] * 3,
         out_specs=vmem,
         scratch_shapes=[
+            pltpu.VMEM(fresh_in.shape, BF16),
+            pltpu.VMEM(fresh_grad.shape, BF16),
+            pltpu.VMEM(stash.shape[1:], BF16),
+            pltpu.VMEM(gain.shape, F32),
+            dma((6,)),
             pltpu.VMEM((2 * units, width), BF16),
             pltpu.VMEM((units, width), BF16),
             pltpu.VMEM((ticks, 2, 2, 8, 2) + tile, BF16),

time: 148 us -> 148 us (level)
  no operation moved by 1% of the time
where the time goes in v3:
time: 148 us
  Pallas kernels  146 us (99%)
    pallas_call x1, Pallas kernels, on_device(): pl.pallas_call(functools.partial(kernel, ticks), out_shape=jax.ShapeDtype...  146 us

profile of v3, /device:TPU:1, one launch (start us, length us, event | category | flops | bytes accessed | tf_op | source)
XLA Modules:
  0.0 147.9 jit_solution(15510987525662996958)
XLA Ops:
  0.6 145.9 %relay.1 = bf16[2,128,128]{2,1,0:T(8,128)(2,1)} custom-call(bf16[1,128,128]{2,1,0:T(8,128)(2,1)} %act.1, bf16[1,128,128]{2,1,0:T(8,128)(2,1)} %grad.1, bf16[2,128,128]{2,1,0:T(8,128)(2,1)} %fresh_f_hbm.1, bf16[2,128,128]{2,1,0:T(8,128)(2,1)} %fresh_b_hbm.1, bf16[1,4,128,128]{3,2,1,0:T(8,128)(2,1)} %stash_hbm.1, s32[3,8]{1,0:T(4,128)} %plan.1, ...), custom_call_target="tpu_custom_call" | custom-call | tf_op jit(solution)/shard_map/relay/pallas_call | solution.py:518
  146.5 1.4 fusion
